TPU v7x, 256 devices: a whole 4x4x8 slice. The times are simulated.
256 devices in a mesh: wide: 32 (over z_hi, x, core), fsdp: 8 (over y, z_lo).
Axes of the slice: x: 4, y: 4, z: 8 (z_hi: 4, z_lo: 2; z = z_hi * 2 + z_lo), core: 2. Of those that a mesh axis runs over, the one named last changes fastest.
Arguments:
- tokens: bfloat16 [8192, 4096], P('wide', 'fsdp'), may hold values from -6 to 6
- norm_gain: float32 [4096], replicated, may hold values from 0.1 to 1.9
- route_ids: int32 [8192, 2], P('wide'), may hold values from 0 to 1, all different within a row
- route_gates: float32 [8192, 2], P('wide'), may hold values from 0.2 to 1
- w_gate: bfloat16 [2, 1536, 4096], P(None, 'fsdp'), may hold values from -0.09375 to 0.09375
- w_up: bfloat16 [2, 1536, 4096], P(None, 'fsdp'), may hold values from -0.09375 to 0.09375
- w_down: bfloat16 [2, 1536, 4096], P(None, 'fsdp'), may hold values from -0.15625 to 0.15625
- a_factors: float32 [2, 3, 64, 4096], P(None, None, 'wide', 'fsdp'), may hold values from -0.09375 to 0.09375
- b_factors: float32 [2, 3, 64, 1536], P(None, None, 'wide', 'fsdp'), may hold values from -0.6 to 0.6
Outputs:
- moe_out: bfloat16 [8192, 4096], P('wide', 'fsdp')
All inputs are finite; a program needn't handle non-finite values.
Results may differ from a plain program's by a relative error of at most 0.017.
Values may be sent and summed in bfloat16 or wider, within the bound.
A program may use at most 64 MiB of HBM per device.

v0:
```python
import jax
import jax.numpy as jnp
from jax import lax
from jax.sharding import PartitionSpec as P

adapter_scale = 2.0


def merge_one(weight_matrix, left, right):
    weight_update = lax.dot_general(
        left,
        right,
        (((0,), (0,)), ((), ())),
        precision=lax.Precision.HIGHEST,
        preferred_element_type=jnp.float32,
    )
    return (weight_matrix.astype(jnp.float32) + adapter_scale * weight_update).astype(jnp.bfloat16)


def project_rows(normed, merged):
    return lax.dot_general(
        normed, merged, (((1,), (1,)), ((), ())), preferred_element_type=jnp.float32
    )


def per_device(
    tokens, norm_gain, route_ids, route_gates, w_gate, w_up, w_down, a_factors, b_factors
):
    a_partial = lax.all_gather(a_factors, "fsdp", axis=3, tiled=True)
    a_whole, full_b_factor = (
        lax.all_gather(a_partial, "wide", axis=2, tiled=True),
        lax.all_gather(b_factors, "wide", axis=2, tiled=True),
    )
    gathered = lax.all_gather(tokens, "fsdp", axis=1, tiled=True)
    value_entries = gathered.astype(jnp.float32)
    mean_square = jnp.mean(value_entries * value_entries, axis=-1, keepdims=True)
    normed = (value_entries * lax.rsqrt(mean_square + 1e-06) * norm_gain).astype(jnp.bfloat16)
    count_experts = w_gate.shape[0]
    labels = jnp.arange(count_experts, dtype=jnp.int32)
    match = (route_ids[:, :, None] == labels[None, None, :]).astype(jnp.float32)
    mix = jnp.sum(match * route_gates[:, :, None], axis=1)
    total = jnp.zeros((gathered.shape[0], gathered.shape[1]), jnp.float32)
    for expert in range(count_experts):
        merged_gate = merge_one(w_gate[expert], full_b_factor[expert, 0], a_whole[expert, 0])
        merged_up = merge_one(w_up[expert], full_b_factor[expert, 1], a_whole[expert, 1])
        merged_down = merge_one(w_down[expert], full_b_factor[expert, 2], a_whole[expert, 2])
        gate_act = project_rows(normed, merged_gate)
        up_act = project_rows(normed, merged_up)
        hidden_state = (jax.nn.silu(gate_act) * up_act * mix[:, expert : expert + 1]).astype(
            jnp.bfloat16
        )
        total = total + jnp.dot(hidden_state, merged_down, preferred_element_type=jnp.float32)
    return lax.psum_scatter(total.astype(jnp.bfloat16), "fsdp", scatter_dimension=1, tiled=True)


def solution(mesh):
    placed = (
        P("wide", "fsdp"),
        P(),
        P("wide", None),
        P("wide", None),
        P(None, "fsdp", None),
        P(None, "fsdp", None),
        P(None, "fsdp", None),
        P(None, None, "wide", "fsdp"),
        P(None, None, "wide", "fsdp"),
    )
    return jax.shard_map(
        per_device, mesh=mesh, in_specs=placed, out_specs=P("wide", "fsdp"), check_vma=False
    )
```

profile of v0, /device:TPU:8, one launch (start us, length us, event | category | flops | bytes accessed | tf_op | source)
XLA Modules:
  0.0 249.4 jit_solution(5624490072889874530)
XLA Ops:
  6.5 0.0 all-gather.3.cloned.1.call-start
  6.5 0.7 all-gather.3.cloned.1.call-update
  7.3 0.0 all-gather.5.cloned.1.call-start
  7.3 0.8 copy.19
  8.1 30.7 %all_gather.14 = f32[2,3,2,4096]{3,0,1,2:T(2,128)} all-gather(f32[2,3,2,512]{3,0,1,2:T(2,128)S(1)} %copy.19), channel_id=1, replica_groups=mesh['wide'=32,'fsdp'=8] {'fsdp'}, dimensions={3}, use_global_device_ids=true | all-gather | bytes 221184 | tf_op jit(solution)/shard_map/all_gather | solution.py:29
  38.8 0.0 all-gather.5.cloned.1.call-update
  38.8 0.0 reduce-scatter.2.cloned.1.call-start
  38.9 0.7 copy.18
  39.6 0.7 fusion.59
  40.3 47.7 %all_gather.13 = f32[2,3,64,192]{3,0,1,2:T(2,128)S(1)} all-gather(f32[2,3,2,192]{3,0,1,2:T(2,128)S(1)} %copy.18), channel_id=1, replica_groups=mesh['wide'=32,'fsdp'=8] {'wide'}, dimensions={2}, use_global_device_ids=true | all-gather | bytes 304128 | tf_op jit(solution)/shard_map/all_gather | solution.py:32
  88.0 0.3 fusion.71
  88.3 0.0 all-gather.3.cloned.1.call-done
  88.3 2.1 fusion.13
  90.4 0.0 copy-start.1
  90.4 51.4 %all-gather.5.cloned.1.call-done = f32[2,3,64,4096]{3,0,1,2:T(2,128)} async-done(((f32[2,3,2,4096]{3,0,1,2:T(2,128)}), f32[2,3,64,4096]{3,0,1,2:T(2,128)}) %all-gather.5.cloned.1.call-update) | async-done | bytes 6291472 | tf_op jit(solution)/shard_map/all_gather | solution.py:31
  141.8 10.9 %fusion.70 = (f32[1,1,64,4096]{3,0,1,2:T(1,128)S(1)}, f32[1,1,64,4096]{3,0,1,2:T(1,128)S(1)}, f32[1,1,64,4096]{3,0,1,2:T(1,128)S(1)}, f32[1,1,64,4096]{3,0,1,2:T...) fusion(f32[2,3,64,4096]{3,0,1,2:T(2,128)} %all-gather.5.cloned.1.call-done), kind=kLoop, calls=%fused_computation.77 | loop fusion | bytes 12582912 | tf_op jit(solution)/shard_map/slice | solution.py:44
  152.7 0.0 copy-done.1
  152.8 3.1 %fusion.12 = bf16[192,4096]{1,0:T(8,128)(2,1)S(1)} fusion(bf16[2,192,4096]{2,1,0:T(8,128)(2,1)S(1)} %copy-done.1, f32[1,1,64,4096]{3,0,1,2:T(1,128)S(1)} %get-tuple-element.10, f32[1,1,64,192]{3,0,1,2:T(1,128)S(1)} %get-tuple-element.16), kind=kOutput, calls=%fused_computation.21 | convolution fusion | flops 607125504 | bytes 4243456 | tf_op jit(solution)/shard_map/dot_general | solution.py:10
  155.9 0.0 copy-start.2
  155.9 3.1 %fusion.9 = bf16[192,4096]{1,0:T(8,128)(2,1)S(1)} fusion(bf16[2,192,4096]{2,1,0:T(8,128)(2,1)S(1)} %copy-done.1, f32[1,1,64,4096]{3,0,1,2:T(1,128)S(1)} %get-tuple-element.5, f32[1,1,64,192]{3,0,1,2:T(1,128)S(1)} %get-tuple-element.11), kind=kOutput, calls=%fused_computation.18 | convolution fusion | flops 607125504 | bytes 4243456 | tf_op jit(solution)/shard_map/dot_general | solution.py:10
  159.1 0.0 copy-done.2
  159.1 4.2 %fusion.10 = bf16[192,4096]{1,0:T(8,128)(2,1)} fusion(bf16[2,192,4096]{2,1,0:T(8,128)(2,1)S(1)} %copy-done.2, f32[1,1,64,4096]{3,0,1,2:T(1,128)S(1)} %get-tuple-element.8, f32[1,1,64,192]{3,0,1,2:T(1,128)S(1)} %get-tuple-element.14), kind=kOutput, calls=%fused_computation.19 | convolution fusion | flops 607125504 | bytes 4243456 | tf_op jit(solution)/shard_map/dot_general | solution.py:10
  163.3 0.0 copy-start.3
  163.3 4.2 %fusion.7 = bf16[192,4096]{1,0:T(8,128)(2,1)} fusion(bf16[2,192,4096]{2,1,0:T(8,128)(2,1)S(1)} %copy-done.2, f32[1,1,64,4096]{3,0,1,2:T(1,128)S(1)} %get-tuple-element.6, f32[1,1,64,192]{3,0,1,2:T(1,128)S(1)} %get-tuple-element.12), kind=kOutput, calls=%fused_computation.16 | convolution fusion | flops 607125504 | bytes 4243456 | tf_op jit(solution)/shard_map/dot_general | solution.py:10
  167.4 0.0 copy-done.3
  167.4 4.2 %fusion.11 = bf16[192,4096]{1,0:T(8,128)(2,1)} fusion(bf16[2,192,4096]{2,1,0:T(8,128)(2,1)S(1)} %copy-done.3, f32[1,1,64,4096]{3,0,1,2:T(1,128)S(1)} %get-tuple-element.9, f32[1,1,64,192]{3,0,1,2:T(1,128)S(1)} %get-tuple-element.15), kind=kOutput, calls=%fused_computation.20 | convolution fusion | flops 607125504 | bytes 4243456 | tf_op jit(solution)/shard_map/dot_general | solution.py:10
  171.6 0.0 copy-start
  171.6 0.0 copy-start.4
  171.6 4.2 %fusion.8 = bf16[192,4096]{1,0:T(8,128)(2,1)} fusion(bf16[2,192,4096]{2,1,0:T(8,128)(2,1)S(1)} %copy-done.3, f32[1,1,64,4096]{3,0,1,2:T(1,128)S(1)} %get-tuple-element.7, f32[1,1,64,192]{3,0,1,2:T(1,128)S(1)} %get-tuple-element.13), kind=kOutput, calls=%fused_computation.17 | convolution fusion | flops 607125504 | bytes 4243456 | tf_op jit(solution)/shard_map/dot_general | solution.py:10
  175.8 0.0 copy-done
  175.8 0.0 copy-done.4
  175.8 0.9 fusion.68
  176.7 0.9 fusion.64
  177.7 6.5 %fusion.20 = f32[256,4096]{1,0:T(8,128)} fusion(bf16[192,4096]{1,0:T(8,128)(2,1)} %fusion.10, bf16[192,4096]{1,0:T(8,128)(2,1)} %fusion.11, f32[256,192]{0,1:T(8,128)S(1)} %fusion.68, f32[256]{0:T(256)S(1)} %bitcast.63, bf16[256,4096]{1,0:T(8,128)(2,1)S(1)} %copy-done, f32[4096]{0:T(1024)S(1)} %copy-done.4, f32[256]{0:T(256)S(1)} %add_rsqrt_fusion), kind=kOutput, calls=%fused_computation.31 | convolution fusion | flops 809844736 | bytes 9652224 | tf_op jit(solution)/shard_map/dot_general | solution.py:52
  184.2 7.1 %fusion.6 = bf16[256,4096]{1,0:T(8,128)(2,1)} fusion(f32[256,4096]{1,0:T(8,128)} %fusion.20, bf16[192,4096]{1,0:T(8,128)(2,1)} %fusion.7, bf16[192,4096]{1,0:T(8,128)(2,1)} %fusion.8, f32[256,192]{0,1:T(8,128)S(1)} %fusion.64, f32[256]{0:T(256)S(1)} %bitcast.62, bf16[256,4096]{1,0:T(8,128)(2,1)S(1)} %copy-done, f32[4096]{0:T(1024)S(1)} %copy-done.4, ...), kind=kOutput, calls=%fused_computation.15 | convolution fusion | flops 811941888 | bytes 11749376 | tf_op jit(solution)/shard_map/dot_general | solution.py:52
  191.3 0.0 reduce-scatter.2.cloned.1.call-update
  191.3 51.6 %reduce-scatter.2.cloned.1.call-done = bf16[256,512]{1,0:T(8,128)(2,1)} async-done(((bf16[256,4096]{1,0:T(8,128)(2,1)}), bf16[256,512]{1,0:T(8,128)(2,1)}) %reduce-scatter.2.cloned.1.call-update) | async-done | bytes 262160 | tf_op jit(solution)/shard_map/reduce_scatter | solution.py:53
  (2 shorter events, 0.0 us)
Async XLA Ops:
  6.5 81.8 %all-gather.3.cloned.1.call-start = ((), (), s32[]{:S(2)}) async-start(), calls=%async_computation.1 | async-start | bytes 2359296 | tf_op jit(solution)/shard_map/all_gather | solution.py:34
  7.3 134.6 %all-gather.5.cloned.1.call-start = ((), (), s32[]{:S(2)}) async-start(), calls=%async_computation.2 | async-start | bytes 6488064 | tf_op jit(solution)/shard_map/all_gather | solution.py:31
  38.8 204.1 %reduce-scatter.2.cloned.1.call-start = ((), (), s32[]{:S(2)}) async-start(), calls=%async_computation.3 | async-start | bytes 2359296 | tf_op jit(solution)/shard_map/reduce_scatter | solution.py:53
  90.4 62.3 %copy-start.1 = (bf16[2,192,4096]{2,1,0:T(8,128)(2,1)S(1)}, bf16[2,192,4096]{2,1,0:T(8,128)(2,1)}, u32[]{:S(2)}) copy-start(bf16[2,192,4096]{2,1,0:T(8,128)(2,1)} %param.13) | copy-start | bytes 9437188
  155.9 3.2 %copy-start.2 = (bf16[2,192,4096]{2,1,0:T(8,128)(2,1)S(1)}, bf16[2,192,4096]{2,1,0:T(8,128)(2,1)}, u32[]{:S(2)}) copy-start(bf16[2,192,4096]{2,1,0:T(8,128)(2,1)} %param.15) | copy-start | bytes 9437188
  163.3 4.2 %copy-start.3 = (bf16[2,192,4096]{2,1,0:T(8,128)(2,1)S(1)}, bf16[2,192,4096]{2,1,0:T(8,128)(2,1)}, u32[]{:S(2)}) copy-start(bf16[2,192,4096]{2,1,0:T(8,128)(2,1)} %param.14) | copy-start | bytes 9437188
  171.6 4.2 %copy-start = (bf16[256,4096]{1,0:T(8,128)(2,1)S(1)}, bf16[256,4096]{1,0:T(8,128)(2,1)}, u32[]{:S(2)}) copy-start(bf16[256,4096]{1,0:T(8,128)(2,1)} %all-gather.3.cloned.1.call-done) | copy-start | bytes 6291460
  171.6 4.2 %copy-start.4 = (f32[4096]{0:T(1024)S(1)}, f32[4096]{0:T(1024)}, u32[]{:S(2)}) copy-start(f32[4096]{0:T(1024)} %param.10) | copy-start | bytes 49156
Sparse Core Ops, SparseCore 0:
  9.1 59.8 all-gather.2
  71.6 70.2 all-gather.4
  191.4 51.4 reduce-scatter.1
where the time goes:
time: 252 us; the launch traced here: 249 us
  waiting for transfers between devices  104 us (41%)
  blocking collectives  78.5 us (31%)
  matrix products  38.5 us (15%)
  between operations  13.2 us (5%)
  local copies, waits for them, and re-layouts  12.7 us (5%)
  other arithmetic  2.8 us (1%)
    reduce_scatter x1, waiting for transfers between devices, per_device(): lax.psum_scatter(total.astype(jnp.bfloat16), 'fsdp', scatter_dimension=1,...  51.6 us
    all_gather x1, waiting for transfers between devices, per_device(): lax.all_gather(a_partial, 'wide', axis=2, tiled=True)  51.4 us
    all_gather x1, blocking collectives, per_device(): lax.all_gather(b_factors, 'wide', axis=2, tiled=True)  47.7 us
    all_gather x1, blocking collectives, per_device(): a_partial = lax.all_gather(a_factors, 'fsdp', axis=3, tiled=True)  30.7 us
    dot_general x6, matrix products, merge_one(): lax.dot_general(left, right, (((0,), (0,)), ((), ())), precision=lax.Prec...  23 us
    dot_general x2, matrix products, per_device(): jnp.dot(hidden_state, merged_down, preferred_element_type=jnp.float32)  13.6 us
    slice x1, local copies, waits for them, and re-layouts, per_device(): a_whole[expert, 0]  10.9 us
  transfers between devices with their start and end apart: 3, of which 2 were waited for; matrix products, arithmetic and copies ran while one was open for 2% of the time, Pallas kernels for 0%

commit v1 on v0

v1 whole, which is shorter than its diff:
```python
import functools

import jax
import jax.numpy as jnp
from jax import lax
from jax.experimental import pallas as pl
from jax.experimental.pallas import tpu as pltpu
from jax.sharding import PartitionSpec as P

F32, BF16 = jnp.float32, jnp.bfloat16
MESH = pl.DeviceIdType.MESH
ROWS, COLS, HID, WIDTH = 256, 512, 192, 4096
HALF, QUART = 128, 64
UB = 32


def dot_nt(a, b):
    return lax.dot_general(a, b, (((1,), (1,)), ((), ())), preferred_element_type=F32)


def dot_nn(a, b):
    return jnp.dot(a, b, preferred_element_type=F32)


def iota(shape, dim):
    return lax.broadcasted_iota(jnp.int32, shape, dim)


def body(
    x_ref, gain_ref, ids_ref, gates_ref, wg_hbm, wu_hbm, wd_hbm, a_ref, b_ref, out_ref,
    w_in, w_down, packet, fac, top, bot, b_exp, bd_t, ad_c,
    xb, acc, sq, hid,
    u_part, u_in, u_blk, u_all, v_part, v_in, v_blk, v_all,
    s1, s2p, s2m, s3, s4p, s4m, s5, r1, r2p, r2m, r3, r4p, r4m, r5,
    wsem, ssem, rsem,
):
    w = lax.axis_index("wide")
    f = lax.axis_index("fsdp")
    zh, xx, core = w // 8, (w // 2) % 4, w % 2
    y, z = f // 2, f % 2

    def fs(dy, flip):
        zz = 1 - z if flip else z
        return ((y + dy) % 4) * 2 + zz

    def wide_at(dzh, dx, dcore):
        return (((zh + dzh) % 4) * 4 + (xx + dx) % 4) * 2 + (core + dcore) % 2

    up, down, across = (w, fs(1, False)), (w, fs(3, False)), (w, fs(0, True))
    count = [0]

    def remote(src, dst, dev):
        i = count[0]
        count[0] += 1
        return pltpu.make_async_remote_copy(
            src_ref=src, dst_ref=dst, send_sem=ssem.at[i], recv_sem=rsem.at[i],
            device_id=dev, device_id_type=MESH,
        )

    loads = []
    for e in range(2):
        for j, (ref, dst) in enumerate(((wg_hbm, w_in.at[pl.ds(e * HID, HID)]),
                                        (wu_hbm, w_in.at[pl.ds((2 + e) * HID, HID)]),
                                        (wd_hbm, w_down.at[pl.ds(e * HID, HID)]))):
            c = pltpu.make_async_copy(ref.at[e], dst, wsem.at[e * 3 + j])
            c.start()
            loads.append(c)

    peers = [(wide_at(d, 0, 0), f) for d in (1, 2, 3)] + [(wide_at(0, d, 0), f) for d in (1, 2, 3)]
    peers += [(wide_at(0, 0, 1), f)] + [(w, (f + i) % 8) for i in range(1, 8)]
    barrier = pltpu.get_barrier_semaphore()
    for p in peers:
        pl.semaphore_signal(barrier, inc=1, device_id=p, device_id_type=MESH)

    packet[...] = jnp.zeros_like(packet)
    for e in range(2):
        for p in range(2):
            r = e * 4 + p * 2
            packet[r:r + 2, 0:512] = a_ref[e, p]
            packet[r:r + 2, 512:704] = b_ref[e, p]
        for h in range(2):
            packet[h * 4 + e * 2:h * 4 + e * 2 + 2, 768:1024] = a_ref[e, 2, :, h * 256:(h + 1) * 256]
        packet[e * 2:e * 2 + 2, 1024:1216] = b_ref[e, 2]
    fac[0, 0, 0] = jnp.concatenate([packet[:, 0:640], packet[:, 640:1280]], axis=0).astype(BF16)

    pl.semaphore_wait(barrier, len(peers))

    def half(ref, h):
        return ref.at[pl.ds(h * HALF, HALF)]

    def quart(ref, h, q):
        return ref.at[pl.ds(h * HALF + q * QUART, QUART)]

    fz = [remote(fac.at[0, 0, 0], fac.at[0, 0, 4 - d], (wide_at(d, 0, 0), f)) for d in (1, 2, 3)]
    fx = [remote(fac.at[0, 0], fac.at[0, 4 - d], (wide_at(0, d, 0), f)) for d in (1, 2, 3)]
    fc = [remote(fac.at[0, d], fac.at[1, d], (wide_at(0, 0, 1), f)) for d in range(4)]
    tok = []
    for h in range(2):
        t = {}
        t["up"] = remote(half(x_ref, h), half(xb.at[0], h), up)
        t["down"] = remote(half(x_ref, h), half(xb.at[1], h), down)
        t["across"] = remote(half(x_ref, h), half(xb.at[2], h), across)
        t["far0"] = remote(quart(xb.at[0], h, 0), quart(xb.at[3], h, 0), up)
        t["far1"] = remote(quart(xb.at[1], h, 1), quart(xb.at[3], h, 1), down)
        t["dup"] = remote(half(xb.at[2], h), half(xb.at[4], h), up)
        t["ddown"] = remote(half(xb.at[2], h), half(xb.at[5], h), down)
        t["dfar"] = remote(half(xb.at[3], h), half(xb.at[6], h), across)
        tok.append(t)
    src = [fs(3, False), fs(1, False), fs(0, True), fs(2, False), fs(3, True), fs(1, True), fs(2, True)]
    other = [(w, (f + i) % 8) for i in range(1, 8)]
    mine = pl.ds(pl.multiple_of(f * UB, UB), UB)

    def rows_of(i):
        return pl.ds(pl.multiple_of(((f + i) % 8) * UB, UB), UB)

    u_rs = [remote(u_part.at[rows_of(i)], u_in.at[i - 1], other[i - 1]) for i in range(1, 8)]
    u_ag = [remote(u_blk, u_all.at[mine], other[i - 1]) for i in range(1, 8)]
    v_rs = [remote(v_part.at[rows_of(i)], v_in.at[i - 1], other[i - 1]) for i in range(1, 8)]
    v_ag = [remote(v_blk, v_all.at[mine], other[i - 1]) for i in range(1, 8)]
    red = []
    for h in range(2):
        t = {}
        t["t1"] = remote(half(s1, h), half(r1, h), across)
        t["t2p"] = remote(half(s2p, h), half(r2m, h), up)
        t["t2m"] = remote(half(s2m, h), half(r2p, h), down)
        t["t3p"] = remote(quart(s3, h, 0), quart(r3, h, 0), up)
        t["t3m"] = remote(quart(s3, h, 1), quart(r3, h, 1), down)
        t["t4p0"] = remote(quart(s4p, h, 0), quart(r4m, h, 0), up)
        t["t4p1"] = remote(quart(s4p, h, 1), quart(r4m, h, 1), up)
        t["t4m0"] = remote(quart(s4m, h, 0), quart(r4p, h, 0), down)
        t["t4m1"] = remote(quart(s4m, h, 1), quart(r4p, h, 1), down)
        t["t5"] = remote(half(s5, h), half(r5, h), across)
        red.append(t)

    def start(h, *names):
        for n in names:
            tok[h][n].start()

    def got(h, *names):
        for n in names:
            tok[h][n].wait_recv()

    def rstart(h, *names):
        for n in names:
            red[h][n].start()

    def rgot(h, *names):
        for n in names:
            red[h][n].wait_recv()

    def scaled(ref, h, owner):
        lanes = pl.ds(pl.multiple_of(owner * COLS, COLS), COLS)
        v = ref[pl.ds(h * HALF, HALF), :].astype(F32)
        s = v * v
        s = (s[:, 0:128] + s[:, 128:256]) + (s[:, 256:384] + s[:, 384:512])
        return (v * gain_ref[:, lanes]).astype(BF16), s, lanes

    def project(ref, h, owner, first=False):
        xg, s, lanes = scaled(ref, h, owner)
        rows = pl.ds(h * HALF, HALF)
        prod = dot_nt(xg, w_in[:, lanes])
        if first:
            acc[rows, :] = prod
            sq[rows, :] = s
        else:
            acc[rows, :] += prod
            sq[rows, :] += s

    def block(h, owner):
        lanes = pl.ds(pl.multiple_of(owner * COLS, COLS), COLS)
        return dot_nn(hid[pl.ds(h * HALF, HALF), :], w_down[:, lanes])

    def activate(h):
        rows = pl.ds(h * HALF, HALF)
        mean = jnp.sum(sq[rows, :], axis=-1, keepdims=True) * (1.0 / WIDTH)
        scale = lax.rsqrt(mean + 1e-06)
        pre = (acc[rows, :] + dot_nn(u_all[rows, :], b_exp[...])) * scale
        g, u = pre[:, 0:2 * HID], pre[:, 2 * HID:4 * HID]
        ids, gates = ids_ref[rows, :], gates_ref[rows, :]
        mix = [jnp.sum(jnp.where(ids == e, gates, 0.0), axis=-1, keepdims=True) for e in range(2)]
        m = jnp.where(iota((HALF, 2 * HID), 1) < HID, mix[0], mix[1])
        hid[rows, :] = (g / (1.0 + jnp.exp(-g)) * u * m).astype(BF16)

    def send_free(h):
        rows = pl.ds(h * HALF, HALF)
        s1[rows, :] = block(h, fs(2, True)).astype(BF16)
        rstart(h, "t1")
        s2p[rows, :] = block(h, fs(1, True)).astype(BF16)
        rstart(h, "t2p")
        s2m[rows, :] = block(h, fs(3, True)).astype(BF16)
        rstart(h, "t2m")
        s4p[rows, :] = block(h, fs(1, False)).astype(BF16)
        rstart(h, "t4p1")
        s4m[rows, :] = block(h, fs(3, False)).astype(BF16)
        rstart(h, "t4m0")

    def send_far(h):
        rows = pl.ds(h * HALF, HALF)
        part = block(h, fs(2, False))
        rgot(h, "t1")
        s3[rows, :] = (part + r1[rows, :].astype(F32)).astype(BF16)
        rstart(h, "t3p", "t3m")

    def send_across(h):
        rows = pl.ds(h * HALF, HALF)
        part = block(h, fs(0, True))
        rgot(h, "t2p", "t2m")
        s5[rows, :] = (part + r2p[rows, :].astype(F32) + r2m[rows, :].astype(F32)).astype(BF16)
        rstart(h, "t5")

    def send_near(h):
        q0, q1 = pl.ds(h * HALF, QUART), pl.ds(h * HALF + QUART, QUART)
        rgot(h, "t3p")
        s4p[q0, :] = (s4p[q0, :].astype(F32) + r3[q0, :].astype(F32)).astype(BF16)
        rstart(h, "t4p0")
        rgot(h, "t3m")
        s4m[q1, :] = (s4m[q1, :].astype(F32) + r3[q1, :].astype(F32)).astype(BF16)
        rstart(h, "t4m1")

    def finish(h):
        rows = pl.ds(h * HALF, HALF)
        part = block(h, f) + dot_nn(v_all[rows, :], ad_c[...])
        rgot(h, "t4p0", "t4p1", "t4m0", "t4m1", "t5")
        part = part + r4p[rows, :].astype(F32) + r4m[rows, :].astype(F32) + r5[rows, :].astype(F32)
        out_ref[rows, :] = part.astype(BF16)

    def exchange_sum(part, arrived, blk, whole, rs, ag):
        total = part[mine, :].astype(F32)
        for i in range(7):
            rs[i].wait_recv()
            total = total + arrived[i].astype(F32)
        blk[...] = total.astype(BF16)
        whole[mine, :] = total.astype(BF16)
        for c in ag:
            c.start()

    for c in fz:
        c.start()
    start(0, "across", "up", "down")
    start(1, "across", "up", "down")
    for c in fz:
        c.wait_recv()
    for c in fx:
        c.start()
    fc[0].start()
    got(0, "across", "up", "down")
    start(0, "far0", "far1", "dup", "ddown")
    for c in loads:
        c.wait()
    project(x_ref, 0, f, True)
    for d in (1, 2, 3):
        fx[3 - d].wait_recv()
        fc[d].start()
    project(x_ref, 1, f, True)
    project(xb.at[2], 0, src[2])
    got(1, "across", "up", "down")
    start(1, "far0", "far1", "dup", "ddown")
    got(0, "far0", "far1")
    start(0, "dfar")
    for c in fc:
        c.wait_recv()

    def unpack(i, carry):
        rows = pl.ds(pl.multiple_of(i * 16, 16), 16)
        two = [fac[i // 8, (i // 2) % 4, (i % 2) * 2 + k].astype(F32) for k in range(2)]
        top[rows, :] = jnp.concatenate([two[0][0:8], two[1][0:8]], axis=0).astype(BF16)
        bot[rows, :] = jnp.concatenate([two[0][8:16], two[1][8:16]], axis=0).astype(BF16)
        return carry

    lax.fori_loop(0, 16, unpack, 0)
    for h in range(2):
        xg, _, _ = scaled(x_ref, h, f)
        u_part[pl.ds(h * HALF, HALF), :] = dot_nt(xg, top[:, 0:512]).astype(BF16)
    for c in u_rs:
        c.start()
    project(xb.at[0], 0, src[0])
    project(xb.at[1], 0, src[1])
    rep = (iota((256, 4 * HID), 0) == iota((256, 4 * HID), 1) % HID).astype(BF16)
    b_in = jnp.concatenate([top[:, 512:640], bot[:, 0:128]], axis=1)
    k, j = iota((256, 4 * HID), 0), iota((256, 4 * HID), 1) // HID
    keep = ((k % 8) // 4 + 2 * ((k % 4) // 2)) == j
    b_exp[...] = jnp.where(keep, 2.0 * dot_nn(b_in, rep), 0.0).astype(BF16)
    got(1, "far0", "far1")
    start(1, "dfar")
    exchange_sum(u_part, u_in, u_blk, u_all, u_rs, u_ag)
    r, k = iota((128, 256), 0), iota((128, 256), 1)
    slot = (r // 4) * 8 + r % 4
    sel0, sel1 = (k == slot).astype(BF16), (k == slot + 4).astype(BF16)
    bd = dot_nn(sel0, bot[:, 384:640]).astype(BF16)
    r, j = iota((128, 2 * HID), 0), iota((128, 2 * HID), 1) // HID
    bd_t[...] = jnp.where((r % 4) // 2 == j, dot_nn(bd, rep[:, 0:2 * HID]), 0.0).astype(BF16)
    ad_c[:, 0:256] = (2.0 * dot_nn(sel0, bot[:, 128:384])).astype(BF16)
    ad_c[:, 256:512] = (2.0 * dot_nn(sel1, bot[:, 128:384])).astype(BF16)
    project(xb.at[3], 0, src[3])
    for i in range(4):
        project(xb.at[i], 1, src[i])
    got(0, "dup", "ddown")
    project(xb.at[4], 0, src[4])
    project(xb.at[5], 0, src[5])
    got(0, "dfar")
    project(xb.at[6], 0, src[6])
    for c in u_ag:
        c.wait_recv()
    activate(0)
    send_free(0)
    got(1, "dup", "ddown")
    project(xb.at[4], 1, src[4])
    project(xb.at[5], 1, src[5])
    got(1, "dfar")
    project(xb.at[6], 1, src[6])
    activate(1)
    v_part[...] = dot_nt(hid[...], bd_t[...]).astype(BF16)
    for c in v_rs:
        c.start()
    send_far(0)
    send_free(1)
    send_across(0)
    exchange_sum(v_part, v_in, v_blk, v_all, v_rs, v_ag)
    send_far(1)
    send_near(0)
    send_across(1)
    for c in v_ag:
        c.wait_recv()
    finish(0)
    send_near(1)
    finish(1)
    for c in fz + fx + fc + u_rs + u_ag + v_rs + v_ag:
        c.wait_send()
    for t in tok + red:
        for c in t.values():
            c.wait_send()


N_COPIES = 3 + 3 + 4 + 16 + 28 + 20


def per_device(tokens, norm_gain, route_ids, route_gates, w_gate, w_up, w_down, a_factors, b_factors):
    vmem = pl.BlockSpec(memory_space=pltpu.VMEM)
    hbm = pl.BlockSpec(memory_space=pl.ANY)
    block = pltpu.VMEM((ROWS, COLS), BF16)
    return pl.pallas_call(
        body,
        out_shape=jax.ShapeDtypeStruct((ROWS, COLS), BF16),
        in_specs=[vmem, vmem, vmem, vmem, hbm, hbm, hbm, vmem, vmem],
        out_specs=vmem,
        scratch_shapes=[
            pltpu.VMEM((4 * HID, WIDTH), BF16),
            pltpu.VMEM((2 * HID, WIDTH), BF16),
            pltpu.VMEM((8, 1280), F32),
            pltpu.VMEM((2, 4, 4, 16, 640), BF16),
            pltpu.VMEM((256, 640), BF16),
            pltpu.VMEM((256, 640), BF16),
            pltpu.VMEM((256, 4 * HID), BF16),
            pltpu.VMEM((128, 2 * HID), BF16),
            pltpu.VMEM((128, COLS), BF16),
            pltpu.VMEM((7, ROWS, COLS), BF16),
            pltpu.VMEM((ROWS, 4 * HID), F32),
            pltpu.VMEM((ROWS, 128), F32),
            pltpu.VMEM((ROWS, 2 * HID), BF16),
            pltpu.VMEM((ROWS, 256), BF16),
            pltpu.VMEM((7, UB, 256), BF16),
            pltpu.VMEM((UB, 256), BF16),
            pltpu.VMEM((ROWS, 256), BF16),
            pltpu.VMEM((ROWS, 128), BF16),
            pltpu.VMEM((7, UB, 128), BF16),
            pltpu.VMEM((UB, 128), BF16),
            pltpu.VMEM((ROWS, 128), BF16),
        ] + [block] * 14 + [
            pltpu.SemaphoreType.DMA((6,)),
            pltpu.SemaphoreType.DMA((N_COPIES,)),
            pltpu.SemaphoreType.DMA((N_COPIES,)),
        ],
        compiler_params=pltpu.CompilerParams(
            collective_id=0, has_side_effects=True, vmem_limit_bytes=48 * 2**20
        ),
    )(tokens, norm_gain.reshape(1, WIDTH), route_ids, route_gates, w_gate, w_up, w_down, a_factors, b_factors)


def solution(mesh):
    placed = (
        P("wide", "fsdp"),
        P(),
        P("wide", None),
        P("wide", None),
        P(None, "fsdp", None),
        P(None, "fsdp", None),
        P(None, "fsdp", None),
        P(None, None, "wide", "fsdp"),
        P(None, None, "wide", "fsdp"),
    )
    return jax.shard_map(
        per_device, mesh=mesh, in_specs=placed, out_specs=P("wide", "fsdp"), check_vma=False
    )
```

time: 252 us -> 60.6 us (0.24)
  the two profiles are of different devices: /device:TPU:8 before, /device:TPU:4 now
where the time goes in v1:
time: 60.6 us; the launch traced here: 60.2 us
  Pallas kernels  52.8 us (87%)
  local copies, waits for them, and re-layouts  7.32 us (12%)
    pallas_call x1, Pallas kernels, per_device(): pl.pallas_call(body, out_shape=jax.ShapeDtypeStruct((ROWS, COLS), BF16),...  52.8 us
    unnamed x13, local copies, waits for them, and re-layouts  7.32 us

profile of v1, /device:TPU:4, one launch (start us, length us, event | category | flops | bytes accessed | tf_op | source)
XLA Modules:
  0.0 60.2 jit_solution(5832072098992650483)
XLA Ops:
  0.0 0.8 %copy.10.ids_ref = s32[256,2]{1,0:T(8,128)S(1)} copy(s32[256,2]{0,1:T(2,128)} %param.11) | data formatting | bytes 4096 | tf_op args[2]
  0.8 0.8 %copy.11.gates_ref = f32[256,2]{1,0:T(8,128)S(1)} copy(f32[256,2]{0,1:T(2,128)} %param.12) | data formatting | bytes 4096 | tf_op args[3]
  1.6 0.0 copy-start
  1.6 1.9 %copy-done = bf16[2,192,4096]{2,1,0:T(8,128)(2,1)S(1)} copy-done((bf16[2,192,4096]{2,1,0:T(8,128)(2,1)S(1)}, bf16[2,192,4096]{2,1,0:T(8,128)(2,1)}, u32[]{:S(2)}) %copy-start) | copy-done | bytes 3145752
  3.5 0.0 copy-start.1
  3.5 0.9 %copy-done.1 = bf16[256,512]{1,0:T(8,128)(2,1)S(1)} copy-done((bf16[256,512]{1,0:T(8,128)(2,1)S(1)}, bf16[256,512]{1,0:T(8,128)(2,1)}, u32[]{:S(2)}) %copy-start.1) | copy-done | bytes 262168
  4.5 0.0 copy-start.2
  4.5 0.7 %copy-done.2 = f32[2,3,2,512]{3,2,1,0:T(2,128)S(1)} copy-done((f32[2,3,2,512]{3,2,1,0:T(2,128)S(1)}, f32[2,3,2,512]{3,2,1,0:T(2,128)}, u32[]{:S(2)}) %copy-start.2) | copy-done | bytes 24600
  5.2 0.0 copy-start.3
  5.2 0.7 %copy-done.3 = f32[4096]{0:T(1024)S(1)} copy-done((f32[4096]{0:T(1024)S(1)}, f32[4096]{0:T(1024)}, u32[]{:S(2)}) %copy-start.3) | copy-done | bytes 16408
  5.9 0.0 copy-start.4
  5.9 0.7 %copy-done.4 = f32[2,3,2,192]{3,2,1,0:T(2,128)S(1)} copy-done((f32[2,3,2,192]{3,2,1,0:T(2,128)S(1)}, f32[2,3,2,192]{3,2,1,0:T(2,128)}, u32[]{:S(2)}) %copy-start.4) | copy-done | bytes 9240
  6.6 52.8 %shard_map.91 = bf16[256,512]{1,0:T(8,128)(2,1)S(1)} custom-call(bf16[256,512]{1,0:T(8,128)(2,1)S(1)} %copy-done.1, f32[1,4096]{1,0:T(1,128)S(1)} %bitcast.1, s32[256,2]{1,0:T(8,128)S(1)} %copy.10.ids_ref, f32[256,2]{1,0:T(8,128)S(1)} %copy.11.gates_ref, bf16[2,192,4096]{2,1,0:T(8,128)(2,1)S(1)} %copy-done, bf16[2,192,4096]{2,1,0:T(8,128)(2,1)} %wu_hbm.1, ...), custom_call_target="tpu_custom_call" | custom-call | tf_op jit(solution)/shard_map/pallas_call | solution.py:341
  59.5 0.7 %copy.13 = bf16[256,512]{1,0:T(8,128)(2,1)} copy(bf16[256,512]{1,0:T(8,128)(2,1)S(1)} %shard_map.91) | data formatting | bytes 524288
Async XLA Ops:
  1.6 1.9 %copy-start = (bf16[2,192,4096]{2,1,0:T(8,128)(2,1)S(1)}, bf16[2,192,4096]{2,1,0:T(8,128)(2,1)}, u32[]{:S(2)}) copy-start(bf16[2,192,4096]{2,1,0:T(8,128)(2,1)} %wg_hbm.1) | copy-start | bytes 9437188
  3.5 0.9 %copy-start.1 = (bf16[256,512]{1,0:T(8,128)(2,1)S(1)}, bf16[256,512]{1,0:T(8,128)(2,1)}, u32[]{:S(2)}) copy-start(bf16[256,512]{1,0:T(8,128)(2,1)} %x_ref.1) | copy-start | bytes 786436
  4.5 0.7 %copy-start.2 = (f32[2,3,2,512]{3,2,1,0:T(2,128)S(1)}, f32[2,3,2,512]{3,2,1,0:T(2,128)}, u32[]{:S(2)}) copy-start(f32[2,3,2,512]{3,2,1,0:T(2,128)} %a_ref.1) | copy-start | bytes 73732
  5.2 0.7 %copy-start.3 = (f32[4096]{0:T(1024)S(1)}, f32[4096]{0:T(1024)}, u32[]{:S(2)}) copy-start(f32[4096]{0:T(1024)} %param.10) | copy-start | bytes 49156
  5.9 0.7 %copy-start.4 = (f32[2,3,2,192]{3,2,1,0:T(2,128)S(1)}, f32[2,3,2,192]{3,2,1,0:T(2,128)}, u32[]{:S(2)}) copy-start(f32[2,3,2,192]{3,2,1,0:T(2,128)} %b_ref.1) | copy-start | bytes 27652

commit v2 on v1

v2 whole, which is shorter than its diff:
```python
import functools

import jax
import jax.numpy as jnp
from jax import lax
from jax.experimental import pallas as pl
from jax.experimental.pallas import tpu as pltpu
from jax.sharding import PartitionSpec as P

F32, BF16 = jnp.float32, jnp.bfloat16
MESH = pl.DeviceIdType.MESH
ROWS, COLS, HID, WIDTH = 256, 512, 192, 4096
HALF, QUART = 128, 64
UB = 32


def dot_nt(a, b):
    return lax.dot_general(a, b, (((1,), (1,)), ((), ())), preferred_element_type=F32)


def dot_nn(a, b):
    return jnp.dot(a, b, preferred_element_type=F32)


def iota(shape, dim):
    return lax.broadcasted_iota(jnp.int32, shape, dim)


def body(
    x_hbm, gain_hbm, ids_hbm, gates_hbm, wg_hbm, wu_hbm, wd_hbm, a_hbm, b_hbm, out_ref,
    x_ref, gain_ref, ids_ref, gates_ref, a_ref, b_ref, w_in, w_down, pack_a, pack_b, fac_a, fac_b, fa, fb, b_exp, bd_t, ad_c, mixed,
    xb, acc, sq, hid,
    u_part, u_in, u_blk, u_all, v_part, v_in, v_blk, v_all,
    s1, s2p, s2m, s3, s4p, s4m, s5, r1, r2p, r2m, r3, r4p, r4m, r5,
    wsem, ssem, rsem,
):
    w = lax.axis_index("wide")
    f = lax.axis_index("fsdp")
    zh, xx, core = w // 8, (w // 2) % 4, w % 2
    y, z = f // 2, f % 2

    def fs(dy, flip):
        zz = 1 - z if flip else z
        return ((y + dy) % 4) * 2 + zz

    def wide_at(dzh, dx, dcore):
        return (((zh + dzh) % 4) * 4 + (xx + dx) % 4) * 2 + (core + dcore) % 2

    up, down, across = (w, fs(1, False)), (w, fs(3, False)), (w, fs(0, True))
    count = [0]

    def remote(src, dst, dev):
        i = count[0]
        count[0] += 1
        return pltpu.make_async_remote_copy(
            src_ref=src, dst_ref=dst, send_sem=ssem.at[i], recv_sem=rsem.at[i],
            device_id=dev, device_id_type=MESH,
        )

    small = [
        pltpu.make_async_copy(src, dst, wsem.at[6 + i])
        for i, (src, dst) in enumerate((
            (a_hbm, a_ref), (b_hbm, b_ref), (x_hbm, x_ref),
            (gain_hbm, gain_ref), (ids_hbm, ids_ref), (gates_hbm, gates_ref),
        ))
    ]
    for c in small:
        c.start()
    loads = []
    for e in range(2):
        for j, (ref, dst) in enumerate(((wg_hbm, w_in.at[pl.ds(e * HID, HID)]),
                                        (wu_hbm, w_in.at[pl.ds((2 + e) * HID, HID)]),
                                        (wd_hbm, w_down.at[pl.ds(e * HID, HID)]))):
            c = pltpu.make_async_copy(ref.at[e], dst, wsem.at[e * 3 + j])
            c.start()
            loads.append(c)

    peers = [(wide_at(d // 2, 0, d % 2), f) for d in range(1, 8)] + [(wide_at(0, d, 0), f) for d in (1, 2, 3)]
    peers += [(w, (f + i) % 8) for i in range(1, 8)]
    barrier = pltpu.get_barrier_semaphore()
    for p in peers:
        pl.semaphore_signal(barrier, inc=1, device_id=p, device_id_type=MESH)

    small[0].wait()
    for e in range(2):
        for p in range(2):
            pack_a[e * 4 + p * 2:e * 4 + p * 2 + 2, :] = a_ref[e, p]
    fac_a[0, 0, 0] = jnp.concatenate([pack_a[:, 0:256], pack_a[:, 256:512]], axis=0).astype(BF16)

    def pack_second():
        pack_b[...] = jnp.zeros_like(pack_b)
        for e in range(2):
            for p in range(2):
                pack_b[e * 4 + p * 2:e * 4 + p * 2 + 2, 0:192] = b_ref[e, p]
            for h in range(2):
                pack_b[h * 4 + e * 2:h * 4 + e * 2 + 2, 256:512] = a_ref[e, 2, :, h * 256:(h + 1) * 256]
            pack_b[e * 2:e * 2 + 2, 512:704] = b_ref[e, 2]
        fac_b[0, 0, 0] = jnp.concatenate([pack_b[:, 0:384], pack_b[:, 384:768]], axis=0).astype(BF16)

    for c in small[1:]:
        c.wait()
    pl.semaphore_wait(barrier, len(peers))

    def half(ref, h):
        return ref.at[pl.ds(h * HALF, HALF)]

    def quart(ref, h, q):
        return ref.at[pl.ds(h * HALF + q * QUART, QUART)]

    near = [(dz, dc) for dc in (0, 1) for dz in (2, 1, 3, 0) if dz or dc]

    def factor_copies(fac):
        by_z = [
            remote(fac.at[0, 0, 0], fac.at[0, dc, (4 - dz) % 4], (wide_at(dz, 0, dc), f)) for dz, dc in near
        ]
        by_x = [remote(fac.at[0], fac.at[4 - d], (wide_at(0, d, 0), f)) for d in (2, 1, 3)]
        return by_z, by_x

    az, ax = factor_copies(fac_a)
    bz, bx = factor_copies(fac_b)
    tok = []
    for h in range(2):
        t = {}
        t["up"] = remote(half(x_ref, h), half(xb.at[0], h), up)
        t["down"] = remote(half(x_ref, h), half(xb.at[1], h), down)
        t["across"] = remote(half(x_ref, h), half(xb.at[2], h), across)
        t["far0"] = remote(quart(xb.at[0], h, 0), quart(xb.at[3], h, 0), up)
        t["far1"] = remote(quart(xb.at[1], h, 1), quart(xb.at[3], h, 1), down)
        t["dup"] = remote(half(xb.at[2], h), half(xb.at[4], h), up)
        t["ddown"] = remote(half(xb.at[2], h), half(xb.at[5], h), down)
        t["dfar"] = remote(half(xb.at[3], h), half(xb.at[6], h), across)
        tok.append(t)
    src = [fs(3, False), fs(1, False), fs(0, True), fs(2, False), fs(3, True), fs(1, True), fs(2, True)]
    other = [(w, (f + i) % 8) for i in range(1, 8)]
    mine = pl.ds(pl.multiple_of(f * UB, UB), UB)

    def rows_of(i):
        return pl.ds(pl.multiple_of(((f + i) % 8) * UB, UB), UB)

    u_rs = [remote(u_part.at[rows_of(i)], u_in.at[i - 1], other[i - 1]) for i in range(1, 8)]
    u_ag = [remote(u_blk, u_all.at[mine], other[i - 1]) for i in range(1, 8)]
    v_rs = [remote(v_part.at[rows_of(i)], v_in.at[i - 1], other[i - 1]) for i in range(1, 8)]
    v_ag = [remote(v_blk, v_all.at[mine], other[i - 1]) for i in range(1, 8)]
    red = []
    for h in range(2):
        t = {}
        t["t1"] = remote(half(s1, h), half(r1, h), across)
        t["t2p"] = remote(half(s2p, h), half(r2m, h), up)
        t["t2m"] = remote(half(s2m, h), half(r2p, h), down)
        t["t3p"] = remote(quart(s3, h, 0), quart(r3, h, 0), up)
        t["t3m"] = remote(quart(s3, h, 1), quart(r3, h, 1), down)
        t["t4p0"] = remote(quart(s4p, h, 0), quart(r4m, h, 0), up)
        t["t4p1"] = remote(quart(s4p, h, 1), quart(r4m, h, 1), up)
        t["t4m0"] = remote(quart(s4m, h, 0), quart(r4p, h, 0), down)
        t["t4m1"] = remote(quart(s4m, h, 1), quart(r4p, h, 1), down)
        t["t5"] = remote(half(s5, h), half(r5, h), across)
        red.append(t)

    def start(h, *names):
        for n in names:
            tok[h][n].start()

    def got(h, *names):
        for n in names:
            tok[h][n].wait_recv()

    def rstart(h, *names):
        for n in names:
            red[h][n].start()

    def rgot(h, *names):
        for n in names:
            red[h][n].wait_recv()

    def scaled(ref, owner):
        lanes = pl.ds(pl.multiple_of(owner * COLS, COLS), COLS)
        v = ref[...].astype(F32)
        s = v * v
        s = (s[:, 0:128] + s[:, 128:256]) + (s[:, 256:384] + s[:, 384:512])
        return (v * gain_ref[:, lanes]).astype(BF16), s, lanes

    def project(ref, owner, first=False):
        xg, s, lanes = scaled(ref, owner)
        prod = dot_nt(xg, w_in[:, lanes])
        if first:
            acc[...] = prod
            sq[...] = s
        else:
            acc[...] += prod
            sq[...] += s

    def block(owner):
        lanes = pl.ds(pl.multiple_of(owner * COLS, COLS), COLS)
        return dot_nn(hid[...], w_down[:, lanes])

    def activate():
        mean = jnp.sum(sq[...], axis=-1, keepdims=True) * (1.0 / WIDTH)
        scale = lax.rsqrt(mean + 1e-06)
        pre = (acc[...] + dot_nn(u_all[...], b_exp[...])) * scale
        g, u = pre[:, 0:2 * HID], pre[:, 2 * HID:4 * HID]
        hid[...] = (g / (1.0 + jnp.exp(-g)) * u * mixed[...]).astype(BF16)

    def mix_rows():
        ids, gates = ids_ref[...], gates_ref[...]
        mix = [jnp.sum(jnp.where(ids == e, gates, 0.0), axis=0, keepdims=True) for e in range(2)]
        r = iota((8, ROWS), 0)
        mix = jnp.where(r == 0, mix[0], jnp.where(r == 1, mix[1], 0.0))
        pick = (iota((8, 2 * HID), 0) == iota((8, 2 * HID), 1) // HID).astype(F32)
        mixed[...] = lax.dot_general(
            mix, pick, (((0,), (0,)), ((), ())), precision=lax.Precision.HIGHEST, preferred_element_type=F32
        )

    def to_block(dst, owner):
        dst[...] = block(owner).astype(BF16)

    def rows_half(h):
        return pl.ds(h * HALF, HALF)

    def send_far(h):
        rows = rows_half(h)
        rgot(h, "t1")
        s3[rows, :] = (s3[rows, :].astype(F32) + r1[rows, :].astype(F32)).astype(BF16)
        rstart(h, "t3p", "t3m")

    def send_across(h):
        rows = rows_half(h)
        rgot(h, "t2p", "t2m")
        s5[rows, :] = (
            s5[rows, :].astype(F32) + r2p[rows, :].astype(F32) + r2m[rows, :].astype(F32)
        ).astype(BF16)
        rstart(h, "t5")

    def send_near(h):
        q0, q1 = pl.ds(h * HALF, QUART), pl.ds(h * HALF + QUART, QUART)
        rgot(h, "t3p")
        s4p[q0, :] = (s4p[q0, :].astype(F32) + r3[q0, :].astype(F32)).astype(BF16)
        rstart(h, "t4p0")
        rgot(h, "t3m")
        s4m[q1, :] = (s4m[q1, :].astype(F32) + r3[q1, :].astype(F32)).astype(BF16)
        rstart(h, "t4m1")

    def finish(h):
        rows = rows_half(h)
        rgot(h, "t5", "t4p1", "t4m0", "t4p0", "t4m1")
        part = acc[rows, 0:COLS] + r4p[rows, :].astype(F32) + r4m[rows, :].astype(F32) + r5[rows, :].astype(F32)
        out_ref[rows, :] = part.astype(BF16)

    def exchange_sum(part, arrived, blk, whole, rs, ag):
        total = part[mine, :].astype(F32)
        for i in range(7):
            rs[i].wait_recv()
            total = total + arrived[i].astype(F32)
        blk[...] = total.astype(BF16)
        whole[mine, :] = total.astype(BF16)
        for c in ag:
            c.start()

    def over_x(by_z, by_x):
        for c in by_z:
            c.wait_recv()
        for c in by_x:
            c.start()

    def unpack(fac, whole, width):
        def step(i, carry):
            rows = pl.ds(pl.multiple_of(i * 16, 16), 16)
            two = [fac[i // 4, (i // 2) % 2, (i % 2) * 2 + k].astype(F32) for k in range(2)]
            whole[rows, 0:width] = jnp.concatenate([two[0][0:8], two[1][0:8]], axis=0).astype(BF16)
            whole[rows, width:2 * width] = jnp.concatenate([two[0][8:16], two[1][8:16]], axis=0).astype(BF16)
            return carry

        lax.fori_loop(0, 16, step, 0)

    def prepare():
        rep = (iota((256, 4 * HID), 0) == iota((256, 4 * HID), 1) % HID).astype(BF16)
        k, j = iota((256, 4 * HID), 0), iota((256, 4 * HID), 1) // HID
        keep = ((k % 8) // 4 + 2 * ((k % 4) // 2)) == j
        b_exp[...] = jnp.where(keep, 2.0 * dot_nn(fb[:, 0:256], rep), 0.0).astype(BF16)
        r, k = iota((128, 256), 0), iota((128, 256), 1)
        slot = (r // 4) * 8 + r % 4
        sel0, sel1 = (k == slot).astype(BF16), (k == slot + 4).astype(BF16)
        bd = dot_nn(sel0, fb[:, 512:768]).astype(BF16)
        r, j = iota((128, 2 * HID), 0), iota((128, 2 * HID), 1) // HID
        bd_t[...] = jnp.where((r % 4) // 2 == j, dot_nn(bd, rep[:, 0:2 * HID]), 0.0).astype(BF16)
        ad_c[:, 0:256] = (2.0 * dot_nn(sel0, fb[:, 256:512])).astype(BF16)
        ad_c[:, 256:512] = (2.0 * dot_nn(sel1, fb[:, 256:512])).astype(BF16)

    for c in az:
        c.start()
    start(0, "up", "down", "across")
    start(1, "up", "down", "across")
    pack_second()
    for c in bz:
        c.start()
    for c in loads:
        c.wait()
    project(x_ref, f, True)
    mix_rows()
    over_x(az, ax)
    got(0, "up")
    start(0, "far0")
    got(0, "down")
    start(0, "far1")
    got(1, "up")
    start(1, "far0")
    got(1, "down")
    start(1, "far1")
    project(xb.at[0], src[0])
    got(0, "across")
    start(0, "dup", "ddown")
    for c in ax:
        c.wait_recv()
    unpack(fac_a, fa, 256)
    xg, _, _ = scaled(x_ref, f)
    u_part[...] = dot_nt(xg, fa[...]).astype(BF16)
    for c in u_rs:
        c.start()
    got(1, "across")
    start(1, "dup", "ddown")
    got(0, "far0", "far1")
    start(0, "dfar")
    over_x(bz, bx)
    got(1, "far0", "far1")
    start(1, "dfar")
    project(xb.at[1], src[1])
    project(xb.at[2], src[2])
    exchange_sum(u_part, u_in, u_blk, u_all, u_rs, u_ag)
    project(xb.at[3], src[3])
    for c in bx:
        c.wait_recv()
    unpack(fac_b, fb, 384)
    prepare()
    got(0, "dup", "ddown")
    got(1, "dup", "ddown")
    project(xb.at[4], src[4])
    project(xb.at[5], src[5])
    got(0, "dfar")
    got(1, "dfar")
    project(xb.at[6], src[6])
    for c in u_ag:
        c.wait_recv()
    activate()
    to_block(s1, fs(2, True))
    rstart(0, "t1")
    rstart(1, "t1")
    to_block(s2p, fs(1, True))
    rstart(0, "t2p")
    to_block(s2m, fs(3, True))
    rstart(0, "t2m")
    to_block(s4p, fs(1, False))
    rstart(0, "t4p1")
    to_block(s4m, fs(3, False))
    rstart(0, "t4m0")
    rstart(1, "t2p", "t2m")
    v_part[...] = dot_nt(hid[...], bd_t[...]).astype(BF16)
    for c in v_rs:
        c.start()
    to_block(s3, fs(2, False))
    send_far(0)
    to_block(s5, fs(0, True))
    acc[:, 0:COLS] = block(f)
    send_far(1)
    rstart(1, "t4p1", "t4m0")
    send_across(0)
    send_near(0)
    exchange_sum(v_part, v_in, v_blk, v_all, v_rs, v_ag)
    send_across(1)
    send_near(1)
    for c in v_ag:
        c.wait_recv()
    acc[:, 0:COLS] += dot_nn(v_all[...], ad_c[...])
    finish(0)
    finish(1)
    for c in az + ax + bz + bx + u_rs + u_ag + v_rs + v_ag:
        c.wait_send()
    for t in tok + red:
        for c in t.values():
            c.wait_send()


N_COPIES = 20 + 16 + 28 + 20


def per_device(tokens, norm_gain, route_ids, route_gates, w_gate, w_up, w_down, a_factors, b_factors):
    vmem = pl.BlockSpec(memory_space=pltpu.VMEM)
    hbm = pl.BlockSpec(memory_space=pl.ANY)
    block = pltpu.VMEM((ROWS, COLS), BF16)
    return pl.pallas_call(
        body,
        out_shape=jax.ShapeDtypeStruct((ROWS, COLS), BF16),
        in_specs=[hbm] * 9,
        out_specs=vmem,
        scratch_shapes=[
            pltpu.VMEM((ROWS, COLS), BF16),
            pltpu.VMEM((1, WIDTH), F32),
            pltpu.VMEM((2, ROWS), jnp.int32),
            pltpu.VMEM((2, ROWS), F32),
            pltpu.VMEM((2, 3, 2, COLS), F32),
            pltpu.VMEM((2, 3, 2, HID), F32),
            pltpu.VMEM((4 * HID, WIDTH), BF16),
            pltpu.VMEM((2 * HID, WIDTH), BF16),
            pltpu.VMEM((8, 512), F32),
            pltpu.VMEM((8, 768), F32),
            pltpu.VMEM((4, 2, 4, 16, 256), BF16),
            pltpu.VMEM((4, 2, 4, 16, 384), BF16),
            pltpu.VMEM((256, 512), BF16),
            pltpu.VMEM((256, 768), BF16),
            pltpu.VMEM((256, 4 * HID), BF16),
            pltpu.VMEM((128, 2 * HID), BF16),
            pltpu.VMEM((128, COLS), BF16),
            pltpu.VMEM((ROWS, 2 * HID), F32),
            pltpu.VMEM((7, ROWS, COLS), BF16),
            pltpu.VMEM((ROWS, 4 * HID), F32),
            pltpu.VMEM((ROWS, 128), F32),
            pltpu.VMEM((ROWS, 2 * HID), BF16),
            pltpu.VMEM((ROWS, 256), BF16),
            pltpu.VMEM((7, UB, 256), BF16),
            pltpu.VMEM((UB, 256), BF16),
            pltpu.VMEM((ROWS, 256), BF16),
            pltpu.VMEM((ROWS, 128), BF16),
            pltpu.VMEM((7, UB, 128), BF16),
            pltpu.VMEM((UB, 128), BF16),
            pltpu.VMEM((ROWS, 128), BF16),
        ] + [block] * 14 + [
            pltpu.SemaphoreType.DMA((12,)),
            pltpu.SemaphoreType.DMA((N_COPIES,)),
            pltpu.SemaphoreType.DMA((N_COPIES,)),
        ],
        compiler_params=pltpu.CompilerParams(
            collective_id=0, has_side_effects=True, vmem_limit_bytes=60 * 2**20
        ),
    )(tokens, norm_gain.reshape(1, WIDTH), route_ids.T, route_gates.T, w_gate, w_up, w_down, a_factors, b_factors)


def solution(mesh):
    placed = (
        P("wide", "fsdp"),
        P(),
        P("wide", None),
        P("wide", None),
        P(None, "fsdp", None),
        P(None, "fsdp", None),
        P(None, "fsdp", None),
        P(None, None, "wide", "fsdp"),
        P(None, None, "wide", "fsdp"),
    )
    return jax.shard_map(
        per_device, mesh=mesh, in_specs=placed, out_specs=P("wide", "fsdp"), check_vma=False
    )
```

time: 60.6 us -> 53.8 us (0.89)
  the two profiles are of different devices: /device:TPU:4 before, /device:TPU:8 now
where the time goes in v2:
time: 53.8 us; the launch traced here: 53.7 us
  Pallas kernels  52 us (97%)
  local copies, waits for them, and re-layouts  1.67 us (3%)
    pallas_call x1, Pallas kernels, per_device(): pl.pallas_call(body, out_shape=jax.ShapeDtypeStruct((ROWS, COLS), BF16),...  52 us
    unnamed x1, local copies, waits for them, and re-layouts  1.67 us

profile of v2, /device:TPU:8, one launch (start us, length us, event | category | flops | bytes accessed | tf_op | source)
XLA Modules:
  0.0 53.7 jit_solution(9392511023882488470)
XLA Ops:
  0.0 52.0 %shard_map.91 = bf16[256,512]{1,0:T(8,128)(2,1)} custom-call(bf16[256,512]{1,0:T(8,128)(2,1)} %x_hbm.1, f32[1,4096]{1,0:T(1,128)} %bitcast.3, s32[2,256]{1,0:T(2,128)} %bitcast.4, f32[2,256]{1,0:T(2,128)} %bitcast.5, bf16[2,192,4096]{2,1,0:T(8,128)(2,1)} %wg_hbm.1, bf16[2,192,4096]{2,1,0:T(8,128)(2,1)} %wu_hbm.1, bf16[2,192,4096]{2,1,0:T(8,128)(2,1)} %wd_hbm.1, ...), custom_call_target="tpu_custom_call" | custom-call | tf_op jit(solution)/shard_map/pallas_call | solution.py:388
  52.0 1.7 %copy.11 = bf16[256,512]{1,0:T(8,128)(2,1)} copy(bf16[256,512]{1,0:T(8,128)(2,1)} %shard_map.91) | data formatting | bytes 524288

commit v3 on v2

--- a/solution.py
+++ b/solution.py
@@ -12,6 +12,7 @@
 ROWS, COLS, HID, WIDTH = 256, 512, 192, 4096
 HALF, QUART = 128, 64
 UB = 32
+SHIFT = 32
 
 
 def dot_nt(a, b):
@@ -27,12 +28,12 @@
 
 
 def body(
-    x_hbm, gain_hbm, ids_hbm, gates_hbm, wg_hbm, wu_hbm, wd_hbm, a_hbm, b_hbm, out_ref,
+    x_hbm, gain_hbm, ids_hbm, gates_hbm, wg_hbm, wu_hbm, wd_hbm, a_hbm, b_hbm, out_hbm,
     x_ref, gain_ref, ids_ref, gates_ref, a_ref, b_ref, w_in, w_down, pack_a, pack_b, fac_a, fac_b, fa, fb, b_exp, bd_t, ad_c, mixed,
     xb, acc, sq, hid,
     u_part, u_in, u_blk, u_all, v_part, v_in, v_blk, v_all,
     s1, s2p, s2m, s3, s4p, s4m, s5, r1, r2p, r2m, r3, r4p, r4m, r5,
-    wsem, ssem, rsem,
+    o_buf, r6p, r6m, wsem, ssem, rsem,
 ):
     w = lax.axis_index("wide")
     f = lax.axis_index("fsdp")
@@ -145,8 +146,13 @@
     for h in range(2):
         t = {}
         t["t1"] = remote(half(s1, h), half(r1, h), across)
-        t["t2p"] = remote(half(s2p, h), half(r2m, h), up)
-        t["t2m"] = remote(half(s2m, h), half(r2p, h), down)
+        kept_p = pl.ds(h * HALF, HALF - h * SHIFT)
+        kept_m = pl.ds(h * HALF + h * SHIFT, HALF - h * SHIFT)
+        t["t2p"] = remote(s2p.at[kept_p], r2m.at[kept_p], up)
+        t["t2m"] = remote(s2m.at[kept_m], r2p.at[kept_m], down)
+        if h == 1:
+            t["t6p"] = remote(s2p.at[pl.ds(ROWS - SHIFT, SHIFT)], r6p, across)
+            t["t6m"] = remote(s2m.at[pl.ds(HALF, SHIFT)], r6m, across)
         t["t3p"] = remote(quart(s3, h, 0), quart(r3, h, 0), up)
         t["t3m"] = remote(quart(s3, h, 1), quart(r3, h, 1), down)
         t["t4p0"] = remote(quart(s4p, h, 0), quart(r4m, h, 0), up)
@@ -189,16 +195,17 @@
             acc[...] += prod
             sq[...] += s
 
-    def block(owner):
+    def block(rows, owner):
         lanes = pl.ds(pl.multiple_of(owner * COLS, COLS), COLS)
-        return dot_nn(hid[...], w_down[:, lanes])
-
-    def activate():
-        mean = jnp.sum(sq[...], axis=-1, keepdims=True) * (1.0 / WIDTH)
+        return dot_nn(hid[rows, :], w_down[:, lanes])
+
+    def activate(h):
+        rows = pl.ds(h * HALF, HALF)
+        mean = jnp.sum(sq[rows, :], axis=-1, keepdims=True) * (1.0 / WIDTH)
         scale = lax.rsqrt(mean + 1e-06)
-        pre = (acc[...] + dot_nn(u_all[...], b_exp[...])) * scale
+        pre = (acc[rows, :] + dot_nn(u_all[rows, :], b_exp[...])) * scale
         g, u = pre[:, 0:2 * HID], pre[:, 2 * HID:4 * HID]
-        hid[...] = (g / (1.0 + jnp.exp(-g)) * u * mixed[...]).astype(BF16)
+        hid[rows, :] = (g / (1.0 + jnp.exp(-g)) * u * mixed[rows, :]).astype(BF16)
 
     def mix_rows():
         ids, gates = ids_ref[...], gates_ref[...]
@@ -210,8 +217,8 @@
             mix, pick, (((0,), (0,)), ((), ())), precision=lax.Precision.HIGHEST, preferred_element_type=F32
         )
 
-    def to_block(dst, owner):
-        dst[...] = block(owner).astype(BF16)
+    def to_block(dst, rows, owner):
+        dst[rows, :] = block(rows, owner).astype(BF16)
 
     def rows_half(h):
         return pl.ds(h * HALF, HALF)
@@ -225,9 +232,14 @@
     def send_across(h):
         rows = rows_half(h)
         rgot(h, "t2p", "t2m")
-        s5[rows, :] = (
-            s5[rows, :].astype(F32) + r2p[rows, :].astype(F32) + r2m[rows, :].astype(F32)
-        ).astype(BF16)
+        kept_p = pl.ds(h * HALF, HALF - h * SHIFT)
+        kept_m = pl.ds(h * HALF + h * SHIFT, HALF - h * SHIFT)
+        total = s5[rows, :].astype(F32)
+        low, high = r2m[kept_p, :].astype(F32), r2p[kept_m, :].astype(F32)
+        if h == 1:
+            none = jnp.zeros((SHIFT, COLS), F32)
+            low, high = jnp.concatenate([low, none], axis=0), jnp.concatenate([none, high], axis=0)
+        s5[rows, :] = (total + low + high).astype(BF16)
         rstart(h, "t5")
 
     def send_near(h):
@@ -239,11 +251,14 @@
         s4m[q1, :] = (s4m[q1, :].astype(F32) + r3[q1, :].astype(F32)).astype(BF16)
         rstart(h, "t4m1")
 
+    stores = [pltpu.make_async_copy(half(o_buf, h), half(out_hbm, h), wsem.at[12 + h]) for h in range(2)]
+
     def finish(h):
         rows = rows_half(h)
         rgot(h, "t5", "t4p1", "t4m0", "t4p0", "t4m1")
         part = acc[rows, 0:COLS] + r4p[rows, :].astype(F32) + r4m[rows, :].astype(F32) + r5[rows, :].astype(F32)
-        out_ref[rows, :] = part.astype(BF16)
+        o_buf[rows, :] = part.astype(BF16)
+        stores[h].start()
 
     def exchange_sum(part, arrived, blk, whole, rs, ag):
         total = part[mine, :].astype(F32)
@@ -290,13 +305,13 @@
     start(0, "up", "down", "across")
     start(1, "up", "down", "across")
     pack_second()
-    for c in bz:
-        c.start()
     for c in loads:
         c.wait()
     project(x_ref, f, True)
     mix_rows()
     over_x(az, ax)
+    for c in bz:
+        c.start()
     got(0, "up")
     start(0, "far0")
     got(0, "down")
@@ -305,9 +320,6 @@
     start(1, "far0")
     got(1, "down")
     start(1, "far1")
-    project(xb.at[0], src[0])
-    got(0, "across")
-    start(0, "dup", "ddown")
     for c in ax:
         c.wait_recv()
     unpack(fac_a, fa, 256)
@@ -315,6 +327,8 @@
     u_part[...] = dot_nt(xg, fa[...]).astype(BF16)
     for c in u_rs:
         c.start()
+    got(0, "across")
+    start(0, "dup", "ddown")
     got(1, "across")
     start(1, "dup", "ddown")
     got(0, "far0", "far1")
@@ -322,9 +336,10 @@
     over_x(bz, bx)
     got(1, "far0", "far1")
     start(1, "dfar")
+    project(xb.at[0], src[0])
+    exchange_sum(u_part, u_in, u_blk, u_all, u_rs, u_ag)
     project(xb.at[1], src[1])
     project(xb.at[2], src[2])
-    exchange_sum(u_part, u_in, u_blk, u_all, u_rs, u_ag)
     project(xb.at[3], src[3])
     for c in bx:
         c.wait_recv()
@@ -339,31 +354,36 @@
     project(xb.at[6], src[6])
     for c in u_ag:
         c.wait_recv()
-    activate()
-    to_block(s1, fs(2, True))
-    rstart(0, "t1")
-    rstart(1, "t1")
-    to_block(s2p, fs(1, True))
-    rstart(0, "t2p")
-    to_block(s2m, fs(3, True))
-    rstart(0, "t2m")
-    to_block(s4p, fs(1, False))
-    rstart(0, "t4p1")
-    to_block(s4m, fs(3, False))
-    rstart(0, "t4m0")
-    rstart(1, "t2p", "t2m")
+    both = pl.ds(0, ROWS)
+    for h in range(2):
+        activate(h)
+        to_block(s2p, rows_half(h), fs(1, True))
+        rstart(h, "t2p")
+        to_block(s2m, rows_half(h), fs(3, True))
+        rstart(h, "t2m")
+        to_block(s1, rows_half(h), fs(2, True))
+        rstart(h, "t1")
+        if h == 1:
+            rstart(1, "t6p", "t6m")
     v_part[...] = dot_nt(hid[...], bd_t[...]).astype(BF16)
     for c in v_rs:
         c.start()
-    to_block(s3, fs(2, False))
+    to_block(s3, both, fs(2, False))
+    to_block(s4p, both, fs(1, False))
+    to_block(s4m, both, fs(3, False))
     send_far(0)
-    to_block(s5, fs(0, True))
-    acc[:, 0:COLS] = block(f)
+    rstart(0, "t4p1", "t4m0")
+    to_block(s5, both, fs(0, True))
+    acc[:, 0:COLS] = block(both, f)
+    send_across(0)
     send_far(1)
+    exchange_sum(v_part, v_in, v_blk, v_all, v_rs, v_ag)
+    rgot(1, "t6p", "t6m")
+    last, lead = pl.ds(ROWS - SHIFT, SHIFT), pl.ds(HALF, SHIFT)
+    s4p[last, :] = (s4p[last, :].astype(F32) + r6p[...].astype(F32)).astype(BF16)
+    s4m[lead, :] = (s4m[lead, :].astype(F32) + r6m[...].astype(F32)).astype(BF16)
     rstart(1, "t4p1", "t4m0")
-    send_across(0)
     send_near(0)
-    exchange_sum(v_part, v_in, v_blk, v_all, v_rs, v_ag)
     send_across(1)
     send_near(1)
     for c in v_ag:
@@ -371,6 +391,8 @@
     acc[:, 0:COLS] += dot_nn(v_all[...], ad_c[...])
     finish(0)
     finish(1)
+    for c in stores:
+        c.wait()
     for c in az + ax + bz + bx + u_rs + u_ag + v_rs + v_ag:
         c.wait_send()
     for t in tok + red:
@@ -378,18 +400,17 @@
             c.wait_send()
 
 
-N_COPIES = 20 + 16 + 28 + 20
+N_COPIES = 20 + 16 + 28 + 20 + 2
 
 
 def per_device(tokens, norm_gain, route_ids, route_gates, w_gate, w_up, w_down, a_factors, b_factors):
-    vmem = pl.BlockSpec(memory_space=pltpu.VMEM)
     hbm = pl.BlockSpec(memory_space=pl.ANY)
     block = pltpu.VMEM((ROWS, COLS), BF16)
     return pl.pallas_call(
         body,
         out_shape=jax.ShapeDtypeStruct((ROWS, COLS), BF16),
         in_specs=[hbm] * 9,
-        out_specs=vmem,
+        out_specs=hbm,
         scratch_shapes=[
             pltpu.VMEM((ROWS, COLS), BF16),
             pltpu.VMEM((1, WIDTH), F32),
@@ -421,8 +442,10 @@
             pltpu.VMEM((7, UB, 128), BF16),
             pltpu.VMEM((UB, 128), BF16),
             pltpu.VMEM((ROWS, 128), BF16),
-        ] + [block] * 14 + [
-            pltpu.SemaphoreType.DMA((12,)),
+        ] + [block] * 15 + [
+            pltpu.VMEM((SHIFT, COLS), BF16),
+            pltpu.VMEM((SHIFT, COLS), BF16),
+            pltpu.SemaphoreType.DMA((14,)),
             pltpu.SemaphoreType.DMA((N_COPIES,)),
             pltpu.SemaphoreType.DMA((N_COPIES,)),
         ],

time: 53.8 us -> 52.6 us (0.978)
  Pallas kernels: 52 us -> 50.8 us
    pallas_call x1, Pallas kernels: 52 us -> 50.8 us  [per_device(): pl.pallas_call(body, out_shape=jax.ShapeDtypeStruct((ROWS, COLS), BF16),...]
where the time goes in v3:
time: 52.6 us; the launch traced here: 52.5 us
  Pallas kernels  50.8 us (97%)
  local copies, waits for them, and re-layouts  1.67 us (3%)
    pallas_call x1, Pallas kernels, per_device(): pl.pallas_call(body, out_shape=jax.ShapeDtypeStruct((ROWS, COLS), BF16),...  50.8 us
    unnamed x1, local copies, waits for them, and re-layouts  1.67 us

profile of v3, /device:TPU:8, one launch (start us, length us, event | category | flops | bytes accessed | tf_op | source)
XLA Modules:
  0.0 52.5 jit_solution(10075908427729494116)
XLA Ops:
  0.0 50.8 %shard_map.91 = bf16[256,512]{1,0:T(8,128)(2,1)} custom-call(bf16[256,512]{1,0:T(8,128)(2,1)} %x_hbm.1, f32[1,4096]{1,0:T(1,128)} %bitcast.3, s32[2,256]{1,0:T(2,128)} %bitcast.4, f32[2,256]{1,0:T(2,128)} %bitcast.5, bf16[2,192,4096]{2,1,0:T(8,128)(2,1)} %wg_hbm.1, bf16[2,192,4096]{2,1,0:T(8,128)(2,1)} %wu_hbm.1, bf16[2,192,4096]{2,1,0:T(8,128)(2,1)} %wd_hbm.1, ...), custom_call_target="tpu_custom_call" | custom-call | tf_op jit(solution)/shard_map/pallas_call | solution.py:409
  50.8 1.7 %copy.11 = bf16[256,512]{1,0:T(8,128)(2,1)} copy(bf16[256,512]{1,0:T(8,128)(2,1)} %shard_map.91) | data formatting | bytes 524288

commit v4 on v3

--- a/solution.py
+++ b/solution.py
@@ -12,7 +12,7 @@
 ROWS, COLS, HID, WIDTH = 256, 512, 192, 4096
 HALF, QUART = 128, 64
 UB = 32
-SHIFT = 32
+SHIFT = 48
 
 
 def dot_nt(a, b):
@@ -65,7 +65,15 @@
             (gain_hbm, gain_ref), (ids_hbm, ids_ref), (gates_hbm, gates_ref),
         ))
     ]
-    for c in small:
+    small[0].start()
+
+    peers = [(wide_at(d // 2, 0, d % 2), f) for d in range(1, 8)] + [(wide_at(0, d, 0), f) for d in (1, 2, 3)]
+    peers += [(w, (f + i) % 8) for i in range(1, 8)]
+    barrier = pltpu.get_barrier_semaphore()
+    for p in peers:
+        pl.semaphore_signal(barrier, inc=1, device_id=p, device_id_type=MESH)
+
+    for c in small[1:]:
         c.start()
     loads = []
     for e in range(2):
@@ -76,12 +84,6 @@
             c.start()
             loads.append(c)
 
-    peers = [(wide_at(d // 2, 0, d % 2), f) for d in range(1, 8)] + [(wide_at(0, d, 0), f) for d in (1, 2, 3)]
-    peers += [(w, (f + i) % 8) for i in range(1, 8)]
-    barrier = pltpu.get_barrier_semaphore()
-    for p in peers:
-        pl.semaphore_signal(barrier, inc=1, device_id=p, device_id_type=MESH)
-
     small[0].wait()
     for e in range(2):
         for p in range(2):
@@ -98,8 +100,6 @@
             pack_b[e * 2:e * 2 + 2, 512:704] = b_ref[e, 2]
         fac_b[0, 0, 0] = jnp.concatenate([pack_b[:, 0:384], pack_b[:, 384:768]], axis=0).astype(BF16)
 
-    for c in small[1:]:
-        c.wait()
     pl.semaphore_wait(barrier, len(peers))
 
     def half(ref, h):
@@ -108,16 +108,21 @@
     def quart(ref, h, q):
         return ref.at[pl.ds(h * HALF + q * QUART, QUART)]
 
-    near = [(dz, dc) for dc in (0, 1) for dz in (2, 1, 3, 0) if dz or dc]
+    near = [(dz, dc) for dz in (2, 1, 3, 0) for dc in (0, 1) if dz or dc]
 
     def factor_copies(fac):
         by_z = [
-            remote(fac.at[0, 0, 0], fac.at[0, dc, (4 - dz) % 4], (wide_at(dz, 0, dc), f)) for dz, dc in near
+            remote(fac.at[0, 0, 0], fac.at[0, (4 - dz) % 4, dc], (wide_at(dz, 0, dc), f)) for dz, dc in near
         ]
         by_x = [remote(fac.at[0], fac.at[4 - d], (wide_at(0, d, 0), f)) for d in (2, 1, 3)]
         return by_z, by_x
 
-    az, ax = factor_copies(fac_a)
+    az, _ = factor_copies(fac_a)
+    ax_of = {
+        slot: [remote(fac_a.at[0, slot], fac_a.at[4 - d, slot], (wide_at(0, d, 0), f)) for d in (2, 1, 3)]
+        for slot in (0, 1, 3, 2)
+    }
+    ax = [c for slot in (0, 1, 3, 2) for c in ax_of[slot]]
     bz, bx = factor_copies(fac_b)
     tok = []
     for h in range(2):
@@ -134,6 +139,8 @@
     src = [fs(3, False), fs(1, False), fs(0, True), fs(2, False), fs(3, True), fs(1, True), fs(2, True)]
     other = [(w, (f + i) % 8) for i in range(1, 8)]
     mine = pl.ds(pl.multiple_of(f * UB, UB), UB)
+
+    far_first = (2, 4, 3, 1, 5, 0, 6)
 
     def rows_of(i):
         return pl.ds(pl.multiple_of(((f + i) % 8) * UB, UB), UB)
@@ -267,8 +274,8 @@
             total = total + arrived[i].astype(F32)
         blk[...] = total.astype(BF16)
         whole[mine, :] = total.astype(BF16)
-        for c in ag:
-            c.start()
+        for i in far_first:
+            ag[i].start()
 
     def over_x(by_z, by_x):
         for c in by_z:
@@ -279,7 +286,7 @@
     def unpack(fac, whole, width):
         def step(i, carry):
             rows = pl.ds(pl.multiple_of(i * 16, 16), 16)
-            two = [fac[i // 4, (i // 2) % 2, (i % 2) * 2 + k].astype(F32) for k in range(2)]
+            two = [fac[i // 4, i % 4, k].astype(F32) for k in range(2)]
             whole[rows, 0:width] = jnp.concatenate([two[0][0:8], two[1][0:8]], axis=0).astype(BF16)
             whole[rows, width:2 * width] = jnp.concatenate([two[0][8:16], two[1][8:16]], axis=0).astype(BF16)
             return carry
@@ -302,6 +309,8 @@
 
     for c in az:
         c.start()
+    for c in small[1:]:
+        c.wait()
     start(0, "up", "down", "across")
     start(1, "up", "down", "across")
     pack_second()
@@ -309,7 +318,12 @@
         c.wait()
     project(x_ref, f, True)
     mix_rows()
-    over_x(az, ax)
+    for slot in (0, 1, 3, 2):
+        for c, (dz, dc) in zip(az, near):
+            if (4 - dz) % 4 == slot:
+                c.wait_recv()
+        for c in ax_of[slot]:
+            c.start()
     for c in bz:
         c.start()
     got(0, "up")
@@ -325,8 +339,8 @@
     unpack(fac_a, fa, 256)
     xg, _, _ = scaled(x_ref, f)
     u_part[...] = dot_nt(xg, fa[...]).astype(BF16)
-    for c in u_rs:
-        c.start()
+    for i in far_first:
+        u_rs[i].start()
     got(0, "across")
     start(0, "dup", "ddown")
     got(1, "across")
@@ -366,8 +380,8 @@
         if h == 1:
             rstart(1, "t6p", "t6m")
     v_part[...] = dot_nt(hid[...], bd_t[...]).astype(BF16)
-    for c in v_rs:
-        c.start()
+    for i in far_first:
+        v_rs[i].start()
     to_block(s3, both, fs(2, False))
     to_block(s4p, both, fs(1, False))
     to_block(s4m, both, fs(3, False))
@@ -377,13 +391,13 @@
     acc[:, 0:COLS] = block(both, f)
     send_across(0)
     send_far(1)
-    exchange_sum(v_part, v_in, v_blk, v_all, v_rs, v_ag)
     rgot(1, "t6p", "t6m")
     last, lead = pl.ds(ROWS - SHIFT, SHIFT), pl.ds(HALF, SHIFT)
     s4p[last, :] = (s4p[last, :].astype(F32) + r6p[...].astype(F32)).astype(BF16)
     s4m[lead, :] = (s4m[lead, :].astype(F32) + r6m[...].astype(F32)).astype(BF16)
     rstart(1, "t4p1", "t4m0")
     send_near(0)
+    exchange_sum(v_part, v_in, v_blk, v_all, v_rs, v_ag)
     send_across(1)
     send_near(1)
     for c in v_ag:
@@ -400,7 +414,7 @@
             c.wait_send()
 
 
-N_COPIES = 20 + 16 + 28 + 20 + 2
+N_COPIES = 20 + 16 + 28 + 20 + 2 + 12
 
 
 def per_device(tokens, norm_gain, route_ids, route_gates, w_gate, w_up, w_down, a_factors, b_factors):
@@ -422,8 +436,8 @@
             pltpu.VMEM((2 * HID, WIDTH), BF16),
             pltpu.VMEM((8, 512), F32),
             pltpu.VMEM((8, 768), F32),
-            pltpu.VMEM((4, 2, 4, 16, 256), BF16),
-            pltpu.VMEM((4, 2, 4, 16, 384), BF16),
+            pltpu.VMEM((4, 4, 2, 16, 256), BF16),
+            pltpu.VMEM((4, 4, 2, 16, 384), BF16),
             pltpu.VMEM((256, 512), BF16),
             pltpu.VMEM((256, 768), BF16),
             pltpu.VMEM((256, 4 * HID), BF16),

time: 52.6 us -> 51.7 us (0.983); the launches traced: 52.5 us -> 50.9 us
  Pallas kernels: 50.8 us -> 49.2 us
    pallas_call x1, Pallas kernels: 50.8 us -> 49.2 us  [per_device(): pl.pallas_call(body, out_shape=jax.ShapeDtypeStruct((ROWS, COLS), BF16),...]
where the time goes in v4:
time: 51.7 us; the launch traced here: 50.9 us
  Pallas kernels  49.2 us (95%)
  local copies, waits for them, and re-layouts  1.67 us (3%)
    pallas_call x1, Pallas kernels, per_device(): pl.pallas_call(body, out_shape=jax.ShapeDtypeStruct((ROWS, COLS), BF16),...  49.2 us
    unnamed x1, local copies, waits for them, and re-layouts  1.67 us

profile of v4, /device:TPU:8, one launch (start us, length us, event | category | flops | bytes accessed | tf_op | source)
XLA Modules:
  0.0 50.9 jit_solution(6377981767222058716)
XLA Ops:
  0.0 49.2 %shard_map.91 = bf16[256,512]{1,0:T(8,128)(2,1)} custom-call(bf16[256,512]{1,0:T(8,128)(2,1)} %x_hbm.1, f32[1,4096]{1,0:T(1,128)} %bitcast.3, s32[2,256]{1,0:T(2,128)} %bitcast.4, f32[2,256]{1,0:T(2,128)} %bitcast.5, bf16[2,192,4096]{2,1,0:T(8,128)(2,1)} %wg_hbm.1, bf16[2,192,4096]{2,1,0:T(8,128)(2,1)} %wu_hbm.1, bf16[2,192,4096]{2,1,0:T(8,128)(2,1)} %wd_hbm.1, ...), custom_call_target="tpu_custom_call" | custom-call | tf_op jit(solution)/shard_map/pallas_call | solution.py:423
  49.2 1.7 %copy.11 = bf16[256,512]{1,0:T(8,128)(2,1)} copy(bf16[256,512]{1,0:T(8,128)(2,1)} %shard_map.91) | data formatting | bytes 524288

commit v5 on v4

--- a/solution.py
+++ b/solution.py
@@ -311,8 +311,8 @@
         c.start()
     for c in small[1:]:
         c.wait()
-    start(0, "up", "down", "across")
-    start(1, "up", "down", "across")
+    start(0, "across", "up", "down")
+    start(1, "across", "up", "down")
     pack_second()
     for c in loads:
         c.wait()

time: 51.7 us -> 51.7 us (level)
  no operation moved by 1% of the time
where the time goes in v5:
time: 51.7 us; the launch traced here: 50.9 us
  Pallas kernels  49.2 us (95%)
  local copies, waits for them, and re-layouts  1.67 us (3%)
    pallas_call x1, Pallas kernels, per_device(): pl.pallas_call(body, out_shape=jax.ShapeDtypeStruct((ROWS, COLS), BF16),...  49.2 us
    unnamed x1, local copies, waits for them, and re-layouts  1.67 us

profile of v5, /device:TPU:8, one launch (start us, length us, event | category | flops | bytes accessed | tf_op | source)
XLA Modules:
  0.0 50.9 jit_solution(1208334212682878888)
XLA Ops:
  0.0 49.2 %shard_map.91 = bf16[256,512]{1,0:T(8,128)(2,1)} custom-call(bf16[256,512]{1,0:T(8,128)(2,1)} %x_hbm.1, f32[1,4096]{1,0:T(1,128)} %bitcast.3, s32[2,256]{1,0:T(2,128)} %bitcast.4, f32[2,256]{1,0:T(2,128)} %bitcast.5, bf16[2,192,4096]{2,1,0:T(8,128)(2,1)} %wg_hbm.1, bf16[2,192,4096]{2,1,0:T(8,128)(2,1)} %wu_hbm.1, bf16[2,192,4096]{2,1,0:T(8,128)(2,1)} %wd_hbm.1, ...), custom_call_target="tpu_custom_call" | custom-call | tf_op jit(solution)/shard_map/pallas_call | solution.py:423
  49.2 1.7 %copy.11 = bf16[256,512]{1,0:T(8,128)(2,1)} copy(bf16[256,512]{1,0:T(8,128)(2,1)} %shard_map.91) | data formatting | bytes 524288
